TPU v7x, 512 devices: a whole 4x4x16 slice. The times are simulated.
512 devices in a mesh: row: 32 (over x, y, core), col: 16 (over z).
Axes of the slice: x: 4, y: 4, z: 16, core: 2. Of those that a mesh axis runs over, the one named last changes fastest.
Arguments:
- diag_factor: float32 [1024, 1024], P('row', 'col'), may hold values from -1 to 2.5, as said below
- panel_factor: float32 [16384, 1024], P('row', 'col'), may hold values from -0.046875 to 0.046875
- left_factor: float32 [16384, 8192], P('row', 'col'), may hold values from -0.046875 to 0.046875
- pivot_factor: float32 [1024, 8192], P('row', 'col'), may hold values from -0.1875 to 0.1875
- panel_adjoint: float32 [16384, 1024], P('row', 'col'), may hold values from -6 to 6
- left_adjoint: float32 [16384, 8192], P('row', 'col'), may hold values from -6 to 6
- pivot_adjoint: float32 [1024, 8192], P('row', 'col'), may hold values from -6 to 6
- diag_adjoint: float32 [1024, 1024], P('row', 'col'), may hold values from -6 to 6
Outputs:
- solved_panel: float32 [16384, 1024], P('row', 'col')
- left_out: float32 [16384, 8192], P('row', 'col')
- pivot_out: float32 [1024, 8192], P('row', 'col')
- diag_out: float32 [1024, 1024], P('row', 'col')
Inputs may be any that keep to these rules, and one draw needn't show every extreme that they name: diag_factor is lower triangular: zero above the diagonal, diagonal entries at least 1.
All inputs are finite; a program needn't handle non-finite values.
Results may differ from a plain program's by a relative error of at most 0.000073.
Values sent between devices are 32-bit elements; how exact they have to be, the bound alone decides.
A program may use at most 64 MiB of HBM per device.

v0:
```python
import jax
import jax.numpy as jnp
from jax import lax
from jax.sharding import PartitionSpec as P


def right_solve(tile, source):
    return jax.scipy.linalg.solve_triangular(tile, source.T, trans="T", lower=True).T


def local(
    diag_factor,
    panel_factor,
    left_factor,
    pivot_factor,
    panel_adjoint,
    left_adjoint,
    pivot_adjoint,
    diag_adjoint,
):
    highest = lax.Precision.HIGHEST
    block_width = panel_adjoint.shape[1]
    my_col = lax.axis_index("col")
    my_row = lax.axis_index("row")
    column_block = lax.all_gather(diag_factor, "row", axis=0, tiled=True)
    whole_diag = lax.all_gather(column_block, "col", axis=1, tiled=True)
    full_rows = lax.all_gather(panel_adjoint, "col", axis=1, tiled=True)
    solved = right_solve(whole_diag, full_rows)
    solved_panel = lax.dynamic_slice_in_dim(solved, my_col * block_width, block_width, 1)
    picked = solved
    left_out = left_adjoint - jnp.dot(
        picked,
        lax.all_gather(pivot_factor, "row", axis=0, tiled=True),
        precision=highest,
        preferred_element_type=jnp.float32,
    )
    own_rows = diag_adjoint.shape[0]
    picked = solved
    pivot_sum = lax.psum_scatter(
        jnp.einsum("rk,rc->kc", picked, left_factor, precision=highest),
        "row",
        scatter_dimension=0,
        tiled=True,
    )
    picked = solved
    square_sum = lax.psum_scatter(
        jnp.einsum("rk,rc->kc", picked, panel_factor, precision=highest),
        "row",
        scatter_dimension=0,
        tiled=True,
    )
    pivot_out = pivot_adjoint - pivot_sum
    global_row = my_row * own_rows + lax.broadcasted_iota(jnp.int32, (own_rows, block_width), 0)
    global_col = my_col * block_width + lax.broadcasted_iota(jnp.int32, (own_rows, block_width), 1)
    diag_out = diag_adjoint - jnp.where(global_col <= global_row, square_sum, 0.0)
    return (solved_panel, left_out, pivot_out, diag_out)


def solution(mesh):
    in_specs = (
        P("row", "col"),
        P("row", "col"),
        P("row", "col"),
        P("row", "col"),
        P("row", "col"),
        P("row", "col"),
        P("row", "col"),
        P("row", "col"),
    )
    out_specs = (P("row", "col"), P("row", "col"), P("row", "col"), P("row", "col"))
    return jax.shard_map(local, mesh=mesh, in_specs=in_specs, out_specs=out_specs, check_vma=False)
```

profile of v0, /device:TPU:2, one launch (start us, length us, event | category | flops | bytes accessed | tf_op | source)
XLA Modules:
  0.0 463.6 jit_solution(8965409141635587499)
XLA Ops:
  7.2 27.8 %all_gather.12 = f32[1024,64]{1,0:T(8,128)S(1)} all-gather(f32[32,64]{1,0:T(8,128)} %param.8), channel_id=1, replica_groups=mesh['row'=32,'col'=16] {'row'}, dimensions={0}, use_global_device_ids=true | all-gather | bytes 270336 | tf_op jit(solution)/shard_map/all_gather | solution.py:25
  35.0 0.9 copy.14
  36.0 0.7 all-gather.6.cloned.1.call-update
  36.7 0.7 all-gather.8.cloned.1.call-update
  37.5 77.2 %all-gather.4.cloned.1.call-done = f32[1024,1024]{0,1:T(8,128)} async-done(((f32[1024,64]{0,1:T(8,128)}), f32[1024,1024]{0,1:T(8,128)}) %all-gather.4.cloned.1.call-update) | async-done | bytes 4194320 | tf_op jit(solution)/shard_map/all_gather | solution.py:26
  114.7 4.8 %fusion = f32[1024,1024]{0,1:T(8,128)} fusion(f32[1024,1024]{0,1:T(8,128)} %all-gather.4.cloned.1.call-done), kind=kLoop, calls=%fused_computation.3 | loop fusion | flops 2097152 | bytes 8388608 | tf_op jit(solution)/shard_map/jit(_solve_triangular)/triangular_solve | solution.py:8
  119.5 24.1 %while.1 = (s32[]{:T(128)}, f32[1024,1024]{0,1:T(8,128)}, s32[8,2]{0,1:T(2,128)S(1)}, f32[8,128,128]{2,1,0:T(8,128)S(1)}, s32[]{:T(128)}) while((s32[]{:T(128)}, f32[1024,1024]{0,1:T(8,128)}, s32[8,2]{0,1:T(2,128)S(1)}, f32[8,128,128]{2,1,0:T(8,128)S(1)}, s32[]{:T(128)}) %tuple.28), condition=%wide.while_cond, body=%wide.while_body.sunk | while | flops 2 | bytes 393321 | solution.py:8
  120.1 2.3 dynamic-slice.12
  123.1 2.3 dynamic-slice.12
  126.1 2.3 dynamic-slice.12
  129.1 2.3 dynamic-slice.12
  132.2 2.3 dynamic-slice.12
  135.2 2.3 dynamic-slice.12
  138.2 2.3 dynamic-slice.12
  141.2 2.2 dynamic-slice.12
  143.6 78.6 %custom-call.4 = f32[8,128,128]{1,2,0:T(8,128)S(1)} custom-call(f32[8,128,128]{2,1,0:T(8,128)S(1)} %get-tuple-element.11), custom_call_target="InvertDiagBlocksLowerTriangular" | custom-call | tf_op jit(solution)/shard_map/jit(_solve_triangular)/triangular_solve | solution.py:8
  222.2 1.5 fusion.19
  223.8 1.4 convolution_subtract_fusion.4
  225.5 1.4 convolution_subtract_fusion.3
  227.3 1.6 convolution_subtract_fusion.6
  229.3 1.7 convolution_subtract_fusion.7
  231.4 1.9 convolution_subtract_fusion.2
  233.8 2.0 convolution_subtract_fusion.5
  236.4 2.2 convolution_subtract_fusion.1
  238.6 1.2 convolution_dynamic-update-slice_fusion
  240.1 2.6 fusion.36
  243.0 4.8 %fusion.35 = f32[1024,512]{1,0:T(8,128)} fusion(f32[1024,512]{1,0:T(8,128)S(1)} %constant_dynamic-update-slice_fusion.18, f32[512,512]{1,0:T(8,128)S(1)} %copy-done), kind=kOutput, calls=%fused_computation.85 | convolution fusion | flops 3221225472 | bytes 5242880 | tf_op jit(solution)/shard_map/rk,rc->kc/dot_general | solution.py:40
  248.5 6.3 %convolution_subtract_fusion = f32[512,512]{1,0:T(8,128)} fusion(f32[512,512]{1,0:T(8,128)} %param.13, f32[1024,512]{1,0:T(8,128)S(1)} %constant_dynamic-update-slice_fusion.18, f32[1024,512]{1,0:T(8,128)} %all-gather.8.cloned.1.call-done), kind=kOutput, calls=%fused_computation.4 | convolution fusion | flops 3221487616 | bytes 6291456 | tf_op jit(solution)/shard_map/dot_general | solution.py:31
  254.9 95.1 %reduce-scatter.5.cloned.1.call-done = f32[32,64]{1,0:T(8,128)} async-done(((f32[1024,64]{1,0:T(8,128)}), f32[32,64]{1,0:T(8,128)}) %reduce-scatter.5.cloned.1.call-update) | async-done | bytes 8208 | tf_op jit(solution)/shard_map/reduce_scatter | solution.py:46
  349.9 1.4 select_subtract_fusion
  351.3 104.3 %reduce-scatter.3.cloned.1.call-done = f32[32,512]{1,0:T(8,128)} async-done(((f32[1024,512]{1,0:T(8,128)}), f32[32,512]{1,0:T(8,128)}) %reduce-scatter.3.cloned.1.call-update) | async-done | bytes 65552 | tf_op jit(solution)/shard_map/reduce_scatter | solution.py:39
  455.6 1.5 sub.10
  (88 shorter events, 9.4 us)
Async XLA Ops:
  7.2 235.8 %copy-start = (f32[512,512]{1,0:T(8,128)S(1)}, f32[512,512]{1,0:T(8,128)}, u32[]{:S(2)}) copy-start(f32[512,512]{1,0:T(8,128)} %param.10) | copy-start | bytes 3145732
  7.2 107.5 %all-gather.4.cloned.1.call-start = ((), (), s32[]{:S(2)}) async-start(), calls=%async_computation.2 | async-start | bytes 4456448 | tf_op jit(solution)/shard_map/all_gather | solution.py:26
  35.9 186.3 %all-gather.6.cloned.1.call-start = ((), (), s32[]{:S(2)}) async-start(), calls=%async_computation.3 | async-start | bytes 2228224 | tf_op jit(solution)/shard_map/all_gather | solution.py:27
  36.7 211.8 %all-gather.8.cloned.1.call-start = ((), (), s32[]{:S(2)}) async-start(), calls=%async_computation.4 | async-start | bytes 2162688 | tf_op jit(solution)/shard_map/all_gather | solution.py:33
  37.4 312.5 %reduce-scatter.5.cloned.1.call-start = ((), (), s32[]{:S(2)}) async-start(), calls=%async_computation.6 | async-start | bytes 540672 | tf_op jit(solution)/shard_map/reduce_scatter | solution.py:46
  222.2 13.7 %copy-start.2 = (f32[8,128,128]{1,2,0:T(8,128)}, f32[8,128,128]{1,2,0:T(8,128)S(1)}, u32[]{:S(2)}) copy-start(f32[8,128,128]{1,2,0:T(8,128)S(1)} %custom-call.4) | copy-start | bytes 1572868
  222.2 5.1 %copy-start.1 = (f32[512,1024]{0,1:T(8,128)S(1)}, f32[512,1024]{0,1:T(8,128)}, u32[]{:S(2)}) copy-start(f32[512,1024]{0,1:T(8,128)} %all-gather.6.cloned.1.call-done) | copy-start | bytes 6291460
  238.6 1.5 copy-start.3
  242.7 212.9 %reduce-scatter.3.cloned.1.call-start = ((), (), s32[]{:S(2)}) async-start(), calls=%async_computation.5 | async-start | bytes 2162688 | tf_op jit(solution)/shard_map/reduce_scatter | solution.py:39
  248.5 101.4 %copy-start.5 = (f32[32,64]{1,0:T(8,128)S(1)}, f32[32,64]{1,0:T(8,128)}, u32[]{:S(2)}) copy-start(f32[32,64]{1,0:T(8,128)} %param.15) | copy-start | bytes 24580
  248.5 207.1 %copy-start.4 = (f32[32,512]{1,0:T(8,128)S(1)}, f32[32,512]{1,0:T(8,128)}, u32[]{:S(2)}) copy-start(f32[32,512]{1,0:T(8,128)} %param.14) | copy-start | bytes 196612
Sparse Core Ops, SparseCore 0:
  36.0 78.6 all-gather.3
  116.8 70.5 all-gather.5
  190.5 55.6 all-gather.7
  250.3 99.5 reduce-scatter.4
  354.2 101.3 reduce-scatter.2
where the time goes:
time: 465 us; the launch traced here: 464 us
  waiting for transfers between devices  278 us (60%)
  other arithmetic  86.2 us (19%)
  matrix products  30.8 us (7%)
  blocking collectives  27.8 us (6%)
  local copies, waits for them, and re-layouts  25.9 us (6%)
  between operations  14.2 us (3%)
    reduce_scatter x1, waiting for transfers between devices, local(): lax.psum_scatter(jnp.einsum('rk,rc->kc', picked, left_factor, precision=h...  104 us
    reduce_scatter x1, waiting for transfers between devices, local(): lax.psum_scatter(jnp.einsum('rk,rc->kc', picked, panel_factor, precision=...  95.1 us
    another operation x3, other arithmetic, right_solve(): jax.scipy.linalg.solve_triangular(tile, source.T, trans='T', lower=True)  83.4 us
    all_gather x1, waiting for transfers between devices, local(): whole_diag = lax.all_gather(column_block, 'col', axis=1, tiled=True)  77.2 us
    all_gather x1, blocking collectives, local(): column_block = lax.all_gather(diag_factor, 'row', axis=0, tiled=True)  27.8 us
    another operation x40, local copies, waits for them, and re-layouts  23.8 us
    another operation x15, matrix products, right_solve(): jax.scipy.linalg.solve_triangular(tile, source.T, trans='T', lower=True)  17.1 us
  transfers between devices with their start and end apart: 5, of which 3 were waited for; matrix products, arithmetic and copies ran while one was open for 30% of the time, Pallas kernels for 0%

commit v1 on v0

--- a/solution.py
+++ b/solution.py
@@ -23,7 +23,12 @@
     my_col = lax.axis_index("col")
     my_row = lax.axis_index("row")
     column_block = lax.all_gather(diag_factor, "row", axis=0, tiled=True)
-    whole_diag = lax.all_gather(column_block, "col", axis=1, tiled=True)
+    whole_diag = jnp.concatenate(
+        lax.all_to_all(
+            jnp.stack(tuple((column_block for _ in range(lax.psum(1, "col")))), 0), "col", 0, 0
+        ),
+        axis=1,
+    )
     full_rows = lax.all_gather(panel_adjoint, "col", axis=1, tiled=True)
     solved = right_solve(whole_diag, full_rows)
     solved_panel = lax.dynamic_slice_in_dim(solved, my_col * block_width, block_width, 1)

time: 465 us -> 594 us (1.28)
  waiting for transfers between devices: 278 us -> 394 us
  starting transfers between devices: 0.42 us -> 12.8 us
    all_to_all x0 -> x1, waiting for transfers between devices: none -> 202 us  [local(): lax.all_to_all(jnp.stack(tuple((column_block for _ in range(lax.psum(1, '...]
    all_gather x1 -> x0, waiting for transfers between devices: 77.2 us -> none  [local(): whole_diag = lax.all_gather(column_block, 'col', axis=1, tiled=True)]
    all_to_all x0 -> x1, starting transfers between devices: none -> 12.4 us  [local(): lax.all_to_all(jnp.stack(tuple((column_block for _ in range(lax.psum(1, '...]
    reduce_scatter x1, waiting for transfers between devices: 95.1 us -> 85.7 us  [local(): lax.psum_scatter(jnp.einsum('rk,rc->kc', picked, panel_factor, precision=...]
    another operation x40 -> x41, local copies, waits for them, and re-layouts: 23.8 us -> 26.4 us
  transfers between devices with their start and end apart: 5 -> 5, of which waited for: 3 -> 3; matrix products, arithmetic and copies ran while one was open for 30% -> 24% of each run, Pallas kernels for 0% -> 0%
where the time goes in v1:
time: 594 us
  waiting for transfers between devices  394 us (66%)
  other arithmetic  86.3 us (15%)
  matrix products  30.8 us (5%)
  blocking collectives  27.8 us (5%)
  local copies, waits for them, and re-layouts  27.7 us (5%)
  between operations  14.2 us (2%)
  starting transfers between devices  12.8 us (2%)
    all_to_all x1, waiting for transfers between devices, local(): lax.all_to_all(jnp.stack(tuple((column_block for _ in range(lax.psum(1, '...  202 us
    reduce_scatter x1, waiting for transfers between devices, local(): lax.psum_scatter(jnp.einsum('rk,rc->kc', picked, left_factor, precision=h...  104 us
    reduce_scatter x1, waiting for transfers between devices, local(): lax.psum_scatter(jnp.einsum('rk,rc->kc', picked, panel_factor, precision=...  85.7 us
    another operation x3, other arithmetic, right_solve(): jax.scipy.linalg.solve_triangular(tile, source.T, trans='T', lower=True)  83.4 us
    all_gather x1, blocking collectives, local(): column_block = lax.all_gather(diag_factor, 'row', axis=0, tiled=True)  27.8 us
    another operation x40, local copies, waits for them, and re-layouts  23.9 us
    another operation x15, matrix products, right_solve(): jax.scipy.linalg.solve_triangular(tile, source.T, trans='T', lower=True)  17.1 us
    all_to_all x1, starting transfers between devices, local(): lax.all_to_all(jnp.stack(tuple((column_block for _ in range(lax.psum(1, '...  12.4 us
  transfers between devices with their start and end apart: 5, of which 3 were waited for; matrix products, arithmetic and copies ran while one was open for 24% of the time, Pallas kernels for 0%

profile of v1, /device:TPU:2, one launch (start us, length us, event | category | flops | bytes accessed | tf_op | source)
XLA Modules:
  0.0 593.5 jit_solution(3380108188413443091)
XLA Ops:
  7.2 27.8 %all_gather.9 = f32[1024,64]{1,0:T(8,128)S(1)} all-gather(f32[32,64]{1,0:T(8,128)} %param.8), channel_id=1, replica_groups=mesh['row'=32,'col'=16] {'row'}, dimensions={0}, use_global_device_ids=true | all-gather | bytes 270336 | tf_op jit(solution)/shard_map/all_gather | solution.py:25
  35.1 2.5 stack.2
  37.7 12.4 %all-to-all-start = ((f32[16,1024,64]{1,2,0:T(8,128)}), f32[16,1024,64]{1,2,0:T(8,128)}, u32[]{:S(2)}, u32[]{:S(2)}) async-start(f32[16,1024,64]{1,2,0:T(8,128)} %stack.2), calls=%async_computation | async-start | bytes 8388608 | tf_op jit(solution)/shard_map/all_to_all | solution.py:27
  50.8 0.7 all-gather.5.cloned.1.call-update
  51.6 202.3 %all-to-all-done = f32[16,1024,64]{1,2,0:T(8,128)} async-done(((f32[16,1024,64]{1,2,0:T(8,128)}), f32[16,1024,64]{1,2,0:T(8,128)}, u32[]{:S(2)}, u32[]{:S(2)}) %all-to-all-start) | async-done | bytes 4194336 | tf_op jit(solution)/shard_map/all_to_all | solution.py:27
  253.9 4.8 bitcast_select_fusion
  258.7 24.1 %while.1 = (s32[]{:T(128)}, f32[1024,1024]{0,1:T(8,128)}, s32[8,2]{0,1:T(2,128)S(1)}, f32[8,128,128]{2,1,0:T(8,128)S(1)}, s32[]{:T(128)}) while((s32[]{:T(128)}, f32[1024,1024]{0,1:T(8,128)}, s32[8,2]{0,1:T(2,128)S(1)}, f32[8,128,128]{2,1,0:T(8,128)S(1)}, s32[]{:T(128)}) %tuple.27), condition=%wide.while_cond, body=%wide.while_body.sunk | while | flops 2 | bytes 393321 | solution.py:8
  259.3 2.3 dynamic-slice.12
  262.3 2.3 dynamic-slice.12
  265.3 2.3 dynamic-slice.12
  268.4 2.3 dynamic-slice.12
  271.4 2.3 dynamic-slice.12
  274.4 2.3 dynamic-slice.12
  277.4 2.3 dynamic-slice.12
  280.5 2.2 dynamic-slice.12
  282.8 78.6 %custom-call.4 = f32[8,128,128]{1,2,0:T(8,128)S(1)} custom-call(f32[8,128,128]{2,1,0:T(8,128)S(1)} %get-tuple-element.11), custom_call_target="InvertDiagBlocksLowerTriangular" | custom-call | tf_op jit(solution)/shard_map/jit(_solve_triangular)/triangular_solve | solution.py:8
  361.5 1.5 fusion.18
  363.0 1.4 convolution_subtract_fusion.4
  364.7 1.4 convolution_subtract_fusion.3
  366.6 1.6 convolution_subtract_fusion.6
  368.5 1.7 convolution_subtract_fusion.7
  370.7 1.9 convolution_subtract_fusion.2
  373.1 2.0 convolution_subtract_fusion.5
  375.6 2.2 convolution_subtract_fusion.1
  377.9 1.2 convolution_dynamic-update-slice_fusion
  379.3 2.6 fusion.35
  382.2 4.8 fusion.34
  387.8 6.4 %convolution_subtract_fusion = f32[512,512]{1,0:T(8,128)} fusion(f32[512,512]{1,0:T(8,128)} %param.13, f32[1024,512]{1,0:T(8,128)S(1)} %constant_dynamic-update-slice_fusion.18, f32[1024,512]{1,0:T(8,128)} %all-gather.5.cloned.1.call-done), kind=kOutput, calls=%fused_computation.4 | convolution fusion | flops 3221487616 | bytes 6291456 | tf_op jit(solution)/shard_map/dot_general | solution.py:36
  394.1 85.7 %reduce-scatter.5.cloned.1.call-done = f32[32,64]{1,0:T(8,128)} async-done(((f32[1024,64]{1,0:T(8,128)}), f32[32,64]{1,0:T(8,128)}) %reduce-scatter.5.cloned.1.call-update) | async-done | bytes 8208 | tf_op jit(solution)/shard_map/reduce_scatter | solution.py:51
  479.8 1.4 select_subtract_fusion
  481.2 104.3 %reduce-scatter.3.cloned.1.call-done = f32[32,512]{1,0:T(8,128)} async-done(((f32[1024,512]{1,0:T(8,128)}), f32[32,512]{1,0:T(8,128)}) %reduce-scatter.3.cloned.1.call-update) | async-done | bytes 65552 | tf_op jit(solution)/shard_map/reduce_scatter | solution.py:44
  585.5 1.5 sub.10
  (88 shorter events, 10.2 us)
Async XLA Ops:
  7.2 375.1 %copy-start = (f32[512,512]{1,0:T(8,128)S(1)}, f32[512,512]{1,0:T(8,128)}, u32[]{:S(2)}) copy-start(f32[512,512]{1,0:T(8,128)} %param.10) | copy-start | bytes 3145732
  37.7 216.3 %all-to-all-start = ((f32[16,1024,64]{1,2,0:T(8,128)}), f32[16,1024,64]{1,2,0:T(8,128)}, u32[]{:S(2)}, u32[]{:S(2)}) async-start(f32[16,1024,64]{1,2,0:T(8,128)} %stack.2), calls=%async_computation | async-start | bytes 8388608 | tf_op jit(solution)/shard_map/all_to_all | solution.py:27
  50.1 311.4 %all-gather.3.cloned.1.call-start = ((), (), s32[]{:S(2)}) async-start(), calls=%async_computation.3 | async-start | bytes 2228224 | tf_op jit(solution)/shard_map/all_gather | solution.py:32
  50.8 337.0 %all-gather.5.cloned.1.call-start = ((), (), s32[]{:S(2)}) async-start(), calls=%async_computation.4 | async-start | bytes 2162688 | tf_op jit(solution)/shard_map/all_gather | solution.py:38
  51.5 428.3 %reduce-scatter.5.cloned.1.call-start = ((), (), s32[]{:S(2)}) async-start(), calls=%async_computation.6 | async-start | bytes 540672 | tf_op jit(solution)/shard_map/reduce_scatter | solution.py:51
  361.4 13.7 %copy-start.2 = (f32[8,128,128]{1,2,0:T(8,128)}, f32[8,128,128]{1,2,0:T(8,128)S(1)}, u32[]{:S(2)}) copy-start(f32[8,128,128]{1,2,0:T(8,128)S(1)} %custom-call.4) | copy-start | bytes 1572868
  361.5 5.1 copy-start.1
  377.9 1.5 copy-start.3
  381.9 203.6 %reduce-scatter.3.cloned.1.call-start = ((), (), s32[]{:S(2)}) async-start(), calls=%async_computation.5 | async-start | bytes 2162688 | tf_op jit(solution)/shard_map/reduce_scatter | solution.py:44
  387.7 92.1 %copy-start.5 = (f32[32,64]{1,0:T(8,128)S(1)}, f32[32,64]{1,0:T(8,128)}, u32[]{:S(2)}) copy-start(f32[32,64]{1,0:T(8,128)} %param.15) | copy-start | bytes 24580
  387.7 197.8 %copy-start.4 = (f32[32,512]{1,0:T(8,128)S(1)}, f32[32,512]{1,0:T(8,128)}, u32[]{:S(2)}) copy-start(f32[32,512]{1,0:T(8,128)} %param.14) | copy-start | bytes 196612
Sparse Core Ops, SparseCore 0:
  53.0 177.8 all-gather.2
  234.0 76.9 all-gather.4
  382.1 97.7 reduce-scatter.4
  484.1 101.3 reduce-scatter.2
